TPU v7x, 32 devices: a whole 2x2x4 slice. The times are simulated.
32 devices in a mesh: term: 4 (over y, x), sec: 8 (over z, core).
Axes of the slice: x: 2, y: 2, z: 4, core: 2. Of those that a mesh axis runs over, the one named last changes fastest.
Arguments:
- vectors: bfloat16 [1, 512, 256, 256], P(None, 'sec'), may hold values from -6 to 6
- left_env: bfloat16 [4, 16, 256, 256], P('term', 'sec'), may hold values from -0.375 to 0.375
- right_env: bfloat16 [4, 16, 256, 256], P('term', 'sec'), may hold values from -0.375 to 0.375
- left_sector: int32 [8, 64], P('sec'), may hold values from 0 to 1
- right_sector: int32 [8, 64], P('sec'), may hold values from 0 to 1
- tile_count: int32 [8], P('sec'), may hold values from 1 to 64, 384 in all
- departure: int32 [8, 64], P('sec'), may hold values from 0 to 63, each once within a row
- arrival: int32 [8, 64], P('sec'), may hold values from 0 to 63, each once within a row
Outputs:
- sigma: bfloat16 [1, 512, 256, 256], P(None, 'sec', 'term')
Inputs may be any that keep to these rules, and one draw needn't show every extreme that they name: `tile_count`: every sec index owns some tile slots that are live; the busiest left owner has all 64 slots live. `departure`: each row is a permutation of the slots. `arrival`: each row is a permutation of the slots.
All inputs are finite; a program needn't handle non-finite values. No bound on the sum of `tile_count` on one device may be relied on, other than what follows from the above.
Results may differ from a plain program's by a relative error of at most 0.015.
Values may be sent and summed in bfloat16 or wider, within the bound.
A program may use at most 128 MiB of HBM per device.

v0:
```python
import jax
import jax.numpy as jnp
from jax import lax
from jax.sharding import PartitionSpec as P


def pick_blocks(table, index):
    picked = jnp.zeros((index.shape[0],) + table.shape[1:], table.dtype)
    for sector in range(table.shape[0]):
        picked = jnp.where((index == sector)[:, None, None], table[sector][None], picked)
    return picked


def on_device(
    vectors, left_env, right_env, left_sector, right_sector, tile_count, departure, arrival
):
    n_sec = lax.axis_size("sec")
    n_vecs = vectors.shape[0]
    tiles_dev = vectors.shape[1]
    width = vectors.shape[3]
    per_peer = tiles_dev // n_sec
    live = (jnp.arange(tiles_dev, dtype=jnp.int32) < tile_count[0]).astype(jnp.bfloat16)
    masked = vectors * live[None, :, None, None]
    left_blocks = pick_blocks(left_env[0], left_sector[0])
    applied = jnp.einsum(
        "kij,vkjl->vkil", left_blocks, masked, preferred_element_type=jnp.float32
    ).astype(jnp.bfloat16)
    outgoing = jnp.take(applied, departure[0], axis=1)
    outgoing = outgoing.reshape(n_vecs, n_sec, per_peer, width, width)
    incoming = lax.all_to_all(outgoing, "sec", split_axis=1, concat_axis=1, tiled=True)
    incoming = incoming.reshape(n_vecs, tiles_dev, width, width)
    placed = jnp.take(incoming, arrival[0], axis=1)
    right_blocks = pick_blocks(right_env[0], right_sector[0])
    contrib = jnp.einsum(
        "vkil,kml->vkim", placed, right_blocks, preferred_element_type=jnp.float32
    ).astype(jnp.bfloat16)
    summed = lax.psum_scatter(
        contrib.astype(jnp.float32).astype(jnp.bfloat16), "term", scatter_dimension=2, tiled=True
    )
    return summed


def solution(mesh):
    in_specs = (
        P(None, "sec", None, None),
        P("term", "sec", None, None),
        P("term", "sec", None, None),
        P("sec", None),
        P("sec", None),
        P("sec"),
        P("sec", None),
        P("sec", None),
    )
    out_specs = P(None, "sec", "term", None)
    return jax.shard_map(
        on_device, mesh=mesh, in_specs=in_specs, out_specs=out_specs, check_vma=False
    )
```

profile of v0, /device:TPU:9, one launch (start us, length us, event | category | flops | bytes accessed | tf_op | source)
XLA Modules:
  0.0 359.5 jit_solution(374254346802081822)
XLA Ops:
  6.5 0.7 compare_select_fusion.1
  7.2 0.7 compare_and_fusion.1
  7.9 1.0 slice_bitcast_fusion.1
  8.8 0.7 compare_bitcast_fusion.1
  10.2 8.1 %convert_bitcast_fusion.1 = bf16[64,256,256]{1,2,0:T(8,128)(2,1)} fusion(pred[64]{0:T(512)(128)(4,1)S(1)} %get-tuple-element.13, pred[64]{0:T(512)(128)(4,1)S(1)} %get-tuple-element.12, bf16[1,64,256,256]{3,2,1,0:T(8,128)(2,1)} %param.10, bf16[256,256]{1,0:T(8,128)(2,1)S(1)} %get-tuple-element.9, bf16[256,256]{1,0:T(8,128)(2,1)S(1)} %get-tuple-element.8, ...), kind=kOutput, calls=%fused_computation.9 | convolution fusion | flops 2164260864 | bytes 17039616 | tf_op jit(solution)/shard_map/kij,vkjl->vkil/dot_general | solution.py:25
  18.3 8.9 %gather_fusion = bf16[64,256,256]{1,2,0:T(8,128)(2,1)} fusion(bf16[64,256,256]{1,2,0:T(8,128)(2,1)} %convert_bitcast_fusion.1, s32[1024]{0:T(1024)S(1)} %pad_clamp_fusion.1), kind=kCustom, calls=%fused_computation.clone | custom fusion | bytes 16777472 | tf_op jit(solution)/shard_map/jit(_take)/gather | solution.py:28
  27.2 7.5 %bitcast_select_fusion.2 = bf16[1,64,256,256]{2,3,1,0:T(8,128)(2,1)} fusion(bf16[64,256,256]{1,2,0:T(8,128)(2,1)} %gather_fusion, pred[64]{0:T(512)(128)(4,1)S(1)} %compare_and_fusion.1), kind=kLoop, calls=%fused_computation.5 | loop fusion | flops 4194304 | bytes 16777280 | tf_op jit(solution)/shard_map/jit(_take)/select_n | solution.py:28
  34.7 0.0 copy-start.1
  34.7 0.0 copy-start.2
  34.7 0.0 copy-start
  34.7 5.8 %all-to-all-start = ((bf16[1,8,8,256,256]{3,4,2,0,1:T(8,128)(2,1)}), bf16[1,8,8,256,256]{3,4,2,0,1:T(8,128)(2,1)}, u32[]{:S(2)}, u32[]{:S(2)}) async-start(bf16[1,8,8,256,256]{3,4,2,0,1:T(8,128)(2,1)} %bitcast.61), calls=%async_computation | async-start | bytes 16777216 | tf_op jit(solution)/shard_map/all_to_all | solution.py:30
  40.5 0.0 reduce-scatter.2.cloned.1.call-start
  40.5 0.0 copy-done.1
  40.5 0.0 copy-done.2
  40.5 0.0 copy-done
  40.6 180.2 %all-to-all-done = bf16[1,8,8,256,256]{3,4,2,0,1:T(8,128)(2,1)} async-done(((bf16[1,8,8,256,256]{3,4,2,0,1:T(8,128)(2,1)}), bf16[1,8,8,256,256]{3,4,2,0,1:T(8,128)(2,1)}, u32[]{:S(2)}, u32[]{:S(2)}) %all-to-all-start) | async-done | bytes 8388640 | tf_op jit(solution)/shard_map/all_to_all | solution.py:30
  220.8 11.4 %copy.16 = bf16[1,8,8,256,256]{4,3,2,1,0:T(8,128)(2,1)} copy(bf16[1,8,8,256,256]{3,4,2,0,1:T(8,128)(2,1)} %all-to-all-done) | data formatting | bytes 16777216 | tf_op jit(solution)/shard_map/all_to_all | solution.py:30
  232.2 8.9 %gather_fusion.1 = bf16[64,256,256]{2,1,0:T(8,128)(2,1)} fusion(bf16[64,256,256]{2,1,0:T(8,128)(2,1)} %bitcast.62, s32[1024]{0:T(1024)S(1)} %pad_clamp_fusion), kind=kCustom, calls=%fused_computation.1.clone | custom fusion | bytes 16777472 | tf_op jit(solution)/shard_map/jit(_take)/gather | solution.py:32
  241.1 6.9 %convert_bitcast_fusion = bf16[1,64,256,256]{2,3,1,0:T(8,128)(2,1)} fusion(bf16[64,256,256]{2,1,0:T(8,128)(2,1)} %gather_fusion.1, pred[64]{0:T(512)(128)(4,1)S(1)} %compare_and_fusion, pred[64]{0:T(512)(128)(4,1)S(1)} %get-tuple-element.11, pred[64]{0:T(512)(128)(4,1)S(1)} %get-tuple-element.10, bf16[256,256]{1,0:T(8,128)(2,1)S(1)} %get-tuple-element.7, ...), kind=kOutput, calls=%fused_computation.8 | convolution fusion | flops 2164260864 | bytes 17039552 | tf_op jit(solution)/shard_map/vkil,kml->vkim/dot_general | solution.py:34
  248.0 12.3 %copy.17 = bf16[1,64,256,256]{3,1,0,2:T(8,128)(2,1)} copy(bf16[1,64,256,256]{2,3,1,0:T(8,128)(2,1)} %convert_bitcast_fusion) | data formatting | bytes 16777216 | tf_op jit(solution)/shard_map/convert_element_type | solution.py:36
  260.3 0.0 reduce-scatter.2.cloned.1.call-update
  260.4 88.2 %reduce-scatter.2.cloned.1.call-done = bf16[1,64,64,256]{3,1,0,2:T(8,128)(2,1)} async-done(((bf16[1,64,256,256]{3,1,0,2:T(8,128)(2,1)}), bf16[1,64,64,256]{3,1,0,2:T(8,128)(2,1)}) %reduce-scatter.2.cloned.1.call-update) | async-done | bytes 2097168 | tf_op jit(solution)/shard_map/reduce_scatter | solution.py:37
  348.6 4.1 %copy.18 = bf16[1,64,64,256]{3,2,1,0:T(8,128)(2,1)} copy(bf16[1,64,64,256]{3,1,0,2:T(8,128)(2,1)} %reduce-scatter.2.cloned.1.call-done) | data formatting | bytes 4194304 | tf_op jit(solution)/shard_map/reduce_scatter | solution.py:37
  (7 shorter events, 0.1 us)
Async XLA Ops:
  34.7 5.8 %copy-start.1 = (s32[1,64]{1,0:T(1,128)S(1)}, s32[1,64]{1,0:T(1,128)}, u32[]{:S(2)}) copy-start(s32[1,64]{1,0:T(1,128)} %param.17) | copy-start | bytes 772
  34.7 5.8 %copy-start.2 = (s32[1,64]{1,0:T(1,128)S(1)}, s32[1,64]{1,0:T(1,128)}, u32[]{:S(2)}) copy-start(s32[1,64]{1,0:T(1,128)} %param.14) | copy-start | bytes 772
  34.7 5.8 %copy-start = (bf16[1,2,256,256]{3,2,1,0:T(8,128)(2,1)S(1)}, bf16[1,2,256,256]{3,2,1,0:T(8,128)(2,1)}, u32[]{:S(2)}) copy-start(bf16[1,2,256,256]{3,2,1,0:T(8,128)(2,1)} %param.12) | copy-start | bytes 786436
  34.7 186.1 %all-to-all-start = ((bf16[1,8,8,256,256]{3,4,2,0,1:T(8,128)(2,1)}), bf16[1,8,8,256,256]{3,4,2,0,1:T(8,128)(2,1)}, u32[]{:S(2)}, u32[]{:S(2)}) async-start(bf16[1,8,8,256,256]{3,4,2,0,1:T(8,128)(2,1)} %bitcast.61), calls=%async_computation | async-start | bytes 16777216 | tf_op jit(solution)/shard_map/all_to_all | solution.py:30
  40.5 308.1 %reduce-scatter.2.cloned.1.call-start = ((), (), s32[]{:S(2)}) async-start(), calls=%async_computation.2 | async-start | bytes 10485760 | tf_op jit(solution)/shard_map/reduce_scatter | solution.py:37
Sparse Core Ops, SparseCore 0:
  260.5 88.0 reduce-scatter.1
where the time goes:
time: 362 us; the launch traced here: 360 us
  waiting for transfers between devices  268 us (74%)
  local copies, waits for them, and re-layouts  46.7 us (13%)
  matrix products  15 us (4%)
  between operations  14.1 us (4%)
  other arithmetic  9.5 us (3%)
  starting transfers between devices  5.77 us (2%)
    all_to_all x1, waiting for transfers between devices, on_device(): lax.all_to_all(outgoing, 'sec', split_axis=1, concat_axis=1, tiled=True)  180 us
    reduce_scatter x1, waiting for transfers between devices, on_device(): lax.psum_scatter(contrib.astype(jnp.float32).astype(jnp.bfloat16), 'term'...  88.2 us
    convert_element_type x1, local copies, waits for them, and re-layouts, on_device(): contrib = jnp.einsum('vkil,kml->vkim', placed, right_blocks, preferred_el...  12.3 us
    all_to_all x1, local copies, waits for them, and re-layouts, on_device(): lax.all_to_all(outgoing, 'sec', split_axis=1, concat_axis=1, tiled=True)  11.4 us
    gather x1, local copies, waits for them, and re-layouts, on_device(): outgoing = jnp.take(applied, departure[0], axis=1)  8.92 us
    gather x1, local copies, waits for them, and re-layouts, on_device(): placed = jnp.take(incoming, arrival[0], axis=1)  8.92 us
    select_n x2, other arithmetic, on_device(): outgoing = jnp.take(applied, departure[0], axis=1)  8.14 us
    dot_general x1, matrix products, on_device(): jnp.einsum('kij,vkjl->vkil', left_blocks, masked, preferred_element_type=...  8.11 us
  transfers between devices with their start and end apart: 2, of which 2 were waited for; matrix products, arithmetic and copies ran while one was open for 0% of the time, Pallas kernels for 0%

commit v1 on v0

--- a/solution.py
+++ b/solution.py
@@ -1,7 +1,13 @@
+import functools
+
 import jax
 import jax.numpy as jnp
 from jax import lax
+from jax.experimental import pallas as pl
+from jax.experimental.pallas import tpu as pltpu
 from jax.sharding import PartitionSpec as P
+
+MESH = pl.DeviceIdType.MESH
 
 
 def pick_blocks(table, index):
@@ -11,7 +17,26 @@
     return picked
 
 
-def on_device(
+def place_kernel(tiles, arr, recv, out, sem):
+    @pl.loop(0, tiles)
+    def _(s):
+        pltpu.make_async_copy(recv.at[arr[s]], out.at[s], sem).start()
+    pltpu.make_async_copy(recv, out, sem).wait()
+
+
+def place(tiles, order):
+    smem = pl.BlockSpec(memory_space=pltpu.SMEM)
+    hbm = pl.BlockSpec(memory_space=pl.ANY)
+    return pl.pallas_call(
+        functools.partial(place_kernel, tiles.shape[0]),
+        out_shape=jax.ShapeDtypeStruct(tiles.shape, tiles.dtype),
+        in_specs=[smem, hbm],
+        out_specs=hbm,
+        scratch_shapes=[pltpu.SemaphoreType.DMA],
+    )(order, tiles)
+
+
+def many_owners(
     vectors, left_env, right_env, left_sector, right_sector, tile_count, departure, arrival
 ):
     n_sec = lax.axis_size("sec")
@@ -25,19 +50,148 @@
     applied = jnp.einsum(
         "kij,vkjl->vkil", left_blocks, masked, preferred_element_type=jnp.float32
     ).astype(jnp.bfloat16)
-    outgoing = jnp.take(applied, departure[0], axis=1)
+    outgoing = place(applied[0], departure[0])
     outgoing = outgoing.reshape(n_vecs, n_sec, per_peer, width, width)
     incoming = lax.all_to_all(outgoing, "sec", split_axis=1, concat_axis=1, tiled=True)
     incoming = incoming.reshape(n_vecs, tiles_dev, width, width)
-    placed = jnp.take(incoming, arrival[0], axis=1)
+    placed = place(incoming[0], arrival[0])[None]
     right_blocks = pick_blocks(right_env[0], right_sector[0])
     contrib = jnp.einsum(
         "vkil,kml->vkim", placed, right_blocks, preferred_element_type=jnp.float32
     ).astype(jnp.bfloat16)
-    summed = lax.psum_scatter(
-        contrib.astype(jnp.float32).astype(jnp.bfloat16), "term", scatter_dimension=2, tiled=True
-    )
-    return summed
+    return lax.psum_scatter(contrib, "term", scatter_dimension=2, tiled=True)
+
+
+def exchange_kernel(
+    n_sec, n_term, per_peer, rows,
+    dep, lsec, cnt, x_hbm, lq, r, sel_src,
+    recv,
+    x, a, y, out, sel,
+    x_sem, own_sem, s_send, s_recv, o_send, o_recv,
+):
+    me = lax.axis_index("sec")
+    load_x = pltpu.make_async_copy(x_hbm, x, x_sem)
+    load_x.start()
+
+    def peer(step):
+        return lax.rem(me + step, n_sec)
+
+    def sel_copy(to, at):
+        return pltpu.make_async_remote_copy(
+            src_ref=sel_src.at[to], dst_ref=sel.at[at],
+            send_sem=s_send.at[to], recv_sem=s_recv.at[at],
+            device_id={"sec": to}, device_id_type=MESH,
+        )
+
+    def out_copy(to, at):
+        return pltpu.make_async_remote_copy(
+            src_ref=out.at[to], dst_ref=recv.at[at],
+            send_sem=o_send.at[to], recv_sem=o_recv.at[at],
+            device_id={"sec": to}, device_id_type=MESH,
+        )
+
+    barrier = pltpu.get_barrier_semaphore()
+    for step in range(1, n_sec):
+        pl.semaphore_signal(
+            barrier, inc=1, device_id={"sec": peer(step)}, device_id_type=MESH
+        )
+    pl.semaphore_wait(barrier, n_sec - 1)
+
+    for step in range(1, n_sec):
+        sel_copy(peer(step), me).start()
+    sel[me] = sel_src[me]
+    load_x.wait()
+
+    def work(e):
+        @pl.loop(0, per_peer)
+        def _(j):
+            slot = dep[e * per_peer + j]
+            p = jnp.dot(lq[lsec[slot]], x[slot], preferred_element_type=jnp.float32)
+            p = jnp.where(slot < cnt[0], p, 0.0).astype(jnp.bfloat16)
+            for t in range(n_term):
+                a[t, pl.ds(pl.multiple_of(j * rows, rows), rows), :] = p[t * rows:(t + 1) * rows]
+
+        width = x.shape[-1]
+        for s in range(2):
+            total = None
+            for t in range(n_term):
+                part = lax.dot_general(
+                    a[t], r[t, e, s * width:(s + 1) * width, :],
+                    (((1,), (1,)), ((), ())), preferred_element_type=jnp.float32,
+                )
+                total = part if total is None else total + part
+            y[s] = total
+
+        @pl.loop(0, per_peer)
+        def _(j):
+            at = pl.ds(pl.multiple_of(j * rows, rows), rows)
+            second = sel[e, pl.ds(j, 1), :] == 1
+            out[e, at, :] = jnp.where(second, y[1, at, :], y[0, at, :]).astype(jnp.bfloat16)
+
+    @pl.loop(1, n_sec)
+    def _(step):
+        e = peer(step)
+        sel_copy(e, e).wait_recv()
+        work(e)
+        out_copy(e, me).start()
+
+    work(me)
+    own = pltpu.make_async_copy(out.at[me], recv.at[me], own_sem)
+    own.start()
+    for step in range(1, n_sec):
+        e = peer(step)
+        sel_copy(e, me).wait_send()
+        out_copy(e, me).wait_send()
+        out_copy(e, e).wait_recv()
+    own.wait()
+
+
+def on_device(
+    vectors, left_env, right_env, left_sector, right_sector, tile_count, departure, arrival
+):
+    n_sec = lax.axis_size("sec")
+    n_term = lax.axis_size("term")
+    tiles = vectors.shape[1]
+    width = vectors.shape[3]
+    rows = width // n_term
+    per_peer = tiles // n_sec
+    sectors = left_env.shape[1]
+
+    lq = lax.all_to_all(left_env[0], "term", split_axis=1, concat_axis=1, tiled=True)
+    r = lax.all_gather(right_env[0], "sec", axis=0, tiled=True)
+    r = lax.all_gather(r, "term", axis=0, tiled=False)
+    r = r.reshape(n_term, n_sec, sectors * width, width)
+    hits = arrival[0][None, :] == jnp.arange(tiles, dtype=jnp.int32)[:, None]
+    chosen = jnp.sum(jnp.where(hits, right_sector[0][None, :], 0), axis=1).astype(jnp.int32)
+    chosen = jnp.broadcast_to(chosen.reshape(n_sec, per_peer, 1), (n_sec, per_peer, width))
+
+    vmem = pl.BlockSpec(memory_space=pltpu.VMEM)
+    smem = pl.BlockSpec(memory_space=pltpu.SMEM)
+    hbm = pl.BlockSpec(memory_space=pl.ANY)
+    recv = pl.pallas_call(
+        functools.partial(exchange_kernel, n_sec, n_term, per_peer, rows),
+        out_shape=jax.ShapeDtypeStruct((n_sec, per_peer * rows, width), jnp.bfloat16),
+        in_specs=[smem, smem, smem, hbm, vmem, vmem, vmem],
+        out_specs=hbm,
+        scratch_shapes=[
+            pltpu.VMEM((tiles, width, width), jnp.bfloat16),
+            pltpu.VMEM((n_term, per_peer * rows, width), jnp.bfloat16),
+            pltpu.VMEM((2, per_peer * rows, width), jnp.float32),
+            pltpu.VMEM((n_sec, per_peer * rows, width), jnp.bfloat16),
+            pltpu.VMEM((n_sec, per_peer, width), jnp.int32),
+            pltpu.SemaphoreType.DMA,
+            pltpu.SemaphoreType.DMA,
+            pltpu.SemaphoreType.DMA((n_sec,)),
+            pltpu.SemaphoreType.DMA((n_sec,)),
+            pltpu.SemaphoreType.DMA((n_sec,)),
+            pltpu.SemaphoreType.DMA((n_sec,)),
+        ],
+        compiler_params=pltpu.CompilerParams(
+            collective_id=0, has_side_effects=True, vmem_limit_bytes=40 * 1024 * 1024
+        ),
+    )(departure[0], left_sector[0], tile_count, vectors[0], lq, r, chosen)
+    out = place(recv.reshape(tiles, rows, width), arrival[0])
+    return out[None]
 
 
 def solution(mesh):
@@ -52,6 +206,7 @@
         P("sec", None),
     )
     out_specs = P(None, "sec", "term", None)
+    body = on_device if mesh.shape["sec"] <= 8 else many_owners
     return jax.shard_map(
-        on_device, mesh=mesh, in_specs=in_specs, out_specs=out_specs, check_vma=False
+        body, mesh=mesh, in_specs=in_specs, out_specs=out_specs, check_vma=False
     )

time: 362 us -> 266 us (0.73)
  waiting for transfers between devices: 268 us -> 116 us
  Pallas kernels: 0 us -> 126 us
  local copies, waits for them, and re-layouts: 46.7 us -> 5.87 us
  matrix products: 15 us -> 0 us
  other arithmetic: 9.5 us -> 0.11 us
    all_to_all x1, waiting for transfers between devices: 180 us -> 3.85 us  [on_device(): lax.all_to_all(left_env[0], 'term', split_axis=1, concat_axis=1, tiled=True)]
    pallas_call x0 -> x2, Pallas kernels: none -> 126 us  [the longest x1 65.3 us: place(): pl.pallas_call(functools.partial(place_kernel, tiles.shape[0]), out_shape...]
    all_gather x0 -> x2, waiting for transfers between devices: none -> 112 us  [the longest x1 79.4 us: on_device(): r = lax.all_gather(r, 'term', axis=0, tiled=False)]
    reduce_scatter x1 -> x0, waiting for transfers between devices: 88.2 us -> none  [on_device(): lax.psum_scatter(contrib.astype(jnp.float32).astype(jnp.bfloat16), 'term'...]
    gather x2 -> x0, local copies, waits for them, and re-layouts: 17.8 us -> none  [the longest x1 8.92 us: on_device(): outgoing = jnp.take(applied, departure[0], axis=1)]
    dot_general x2 -> x0, matrix products: 15 us -> none  [the longest x1 8.11 us: on_device(): jnp.einsum('kij,vkjl->vkil', left_blocks, masked, preferred_element_type=...]
    convert_element_type x1 -> x0, local copies, waits for them, and re-layouts: 12.3 us -> none  [on_device(): contrib = jnp.einsum('vkil,kml->vkim', placed, right_blocks, preferred_el...]
    all_to_all x1, local copies, waits for them, and re-layouts: 11.4 us -> 0.03 us  [on_device(): lax.all_to_all(left_env[0], 'term', split_axis=1, concat_axis=1, tiled=True)]
  transfers between devices with their start and end apart: 2 -> 3, of which waited for: 2 -> 3; matrix products, arithmetic and copies ran while one was open for 0% -> 0% of each run, Pallas kernels for 0% -> 0%
where the time goes in v1:
time: 266 us
  Pallas kernels  126 us (47%)
  waiting for transfers between devices  116 us (44%)
  between operations  14.1 us (5%)
  local copies, waits for them, and re-layouts  5.87 us (2%)
  starting transfers between devices  3.48 us (1%)
    all_gather x1, waiting for transfers between devices, on_device(): r = lax.all_gather(r, 'term', axis=0, tiled=False)  79.4 us
    pallas_call x1, Pallas kernels, place(): pl.pallas_call(functools.partial(place_kernel, tiles.shape[0]), out_shape...  65.3 us
    pallas_call x1, Pallas kernels, on_device(): pl.pallas_call(functools.partial(exchange_kernel, n_sec, n_term, per_peer...  60.8 us
    all_gather x1, waiting for transfers between devices, on_device(): r = lax.all_gather(right_env[0], 'sec', axis=0, tiled=True)  32.4 us
    unnamed x15, local copies, waits for them, and re-layouts  5.69 us
  transfers between devices with their start and end apart: 3, of which 3 were waited for; matrix products, arithmetic and copies ran while one was open for 0% of the time, Pallas kernels for 0%

profile of v1, /device:TPU:9, one launch (start us, length us, event | category | flops | bytes accessed | tf_op | source)
XLA Modules:
  0.0 266.0 jit_solution(15721505712198391764)
XLA Ops:
  6.5 0.0 copy-start.4
  6.5 0.0 all-gather.5.cloned.1.call-start
  6.6 0.7 all-gather.5.cloned.1.call-update
  7.3 0.0 all-gather.7.cloned.1.call-start
  7.3 32.4 %all-gather.5.cloned.1.call-done = bf16[1,16,256,256]{3,2,0,1:T(8,128)(2,1)} async-done(((bf16[1,2,256,256]{3,2,0,1:T(8,128)(2,1)}), bf16[1,16,256,256]{3,2,0,1:T(8,128)(2,1)}) %all-gather.5.cloned.1.call-update) | async-done | bytes 2097168 | tf_op jit(solution)/shard_map/all_gather | solution.py:161
  39.7 0.0 all-gather.7.cloned.1.call-update
  39.7 0.0 copy-done.4
  39.7 1.0 copy.18
  40.7 3.4 %all-to-all-start = ((bf16[2,256,256]{2,0,1:T(2,128)(2,1)}), bf16[2,256,256]{2,0,1:T(2,128)(2,1)S(1)}, u32[]{:S(2)}, u32[]{:S(2)}) async-start(bf16[2,256,256]{2,0,1:T(2,128)(2,1)} %bitcast.12), calls=%async_computation | async-start | bytes 524288 | tf_op jit(solution)/shard_map/all_to_all | solution.py:160
  44.8 0.0 copy-done.5
  44.8 0.0 copy-done.6
  44.8 0.1 select_reduce_fusion
  44.9 0.1 broadcast_in_dim.28
  45.0 3.8 %all-to-all-done = bf16[2,256,256]{2,0,1:T(2,128)(2,1)S(1)} async-done(((bf16[2,256,256]{2,0,1:T(2,128)(2,1)}), bf16[2,256,256]{2,0,1:T(2,128)(2,1)S(1)}, u32[]{:S(2)}, u32[]{:S(2)}) %all-to-all-start) | async-done | bytes 262176 | tf_op jit(solution)/shard_map/all_to_all | solution.py:160
  48.8 79.4 %all-gather.7.cloned.1.call-done = bf16[4,16,256,256]{3,2,1,0:T(8,128)(2,1)} async-done(((bf16[1,16,256,256]{3,2,1,0:T(8,128)(2,1)}), bf16[4,16,256,256]{3,2,1,0:T(8,128)(2,1)}) %all-gather.7.cloned.1.call-update) | async-done | bytes 8388624 | tf_op jit(solution)/shard_map/all_gather | solution.py:162
  128.3 0.1 broadcast_in_dim.29.sel_src
  128.3 0.0 copy-done.2
  128.3 0.0 copy-done.3
  128.3 0.0 copy-start
  128.4 3.4 %copy-done = bf16[1,64,256,256]{3,2,1,0:T(8,128)(2,1)S(1)} copy-done((bf16[1,64,256,256]{3,2,1,0:T(8,128)(2,1)S(1)}, bf16[1,64,256,256]{3,2,1,0:T(8,128)(2,1)}, u32[]{:S(2)}) %copy-start) | copy-done | bytes 8388632
  131.7 60.8 %shard_map.82 = bf16[8,512,256]{2,1,0:T(8,128)(2,1)S(1)} custom-call(s32[64]{0:T(128)S(1)} %bitcast.15, s32[64]{0:T(128)S(1)} %bitcast.16, s32[1]{0:T(128)S(6)} %copy.19.cnt, bf16[64,256,256]{2,1,0:T(8,128)(2,1)S(1)} %bitcast.13, bf16[2,256,256]{2,1,0:T(8,128)(2,1)S(1)} %copy.16.lq, bf16[4,8,512,256]{3,2,1,0:T(8,128)(2,1)} %bitcast.17, ...), custom_call_target="tpu_custom_call" | custom-call | tf_op jit(solution)/shard_map/pallas_call | solution.py:171
  192.5 0.0 copy-start.1
  192.5 1.3 copy-done.1
  193.9 65.3 %shard_map.83 = bf16[64,64,256]{2,1,0:T(8,128)(2,1)} custom-call(s32[64]{0:T(128)} %bitcast.20, bf16[64,64,256]{2,1,0:T(8,128)(2,1)} %bitcast.14), custom_call_target="tpu_custom_call" | custom-call | tf_op jit(solution)/shard_map/pallas_call | solution.py:30
  (5 shorter events, 0.0 us)
Async XLA Ops:
  6.5 33.2 %copy-start.4 = (bf16[1,2,256,256]{3,2,1,0:T(8,128)(2,1)S(1)}, bf16[1,2,256,256]{3,2,1,0:T(8,128)(2,1)}, u32[]{:S(2)}) copy-start(bf16[1,2,256,256]{3,2,1,0:T(8,128)(2,1)} %param.9) | copy-start | bytes 786436
  6.5 38.2 %copy-start.5 = (s32[1,64]{1,0:T(1,128)S(1)}, s32[1,64]{1,0:T(1,128)}, u32[]{:S(2)}) copy-start(s32[1,64]{1,0:T(1,128)} %param.15) | copy-start | bytes 772
  6.5 38.2 %copy-start.6 = (s32[1,64]{1,0:T(1,128)S(1)}, s32[1,64]{1,0:T(1,128)}, u32[]{:S(2)}) copy-start(s32[1,64]{1,0:T(1,128)} %param.12) | copy-start | bytes 772
  6.5 121.8 %copy-start.2 = (s32[1,64]{1,0:T(1,128)S(1)}, s32[1,64]{1,0:T(1,128)}, u32[]{:S(2)}) copy-start(s32[1,64]{1,0:T(1,128)} %param.14) | copy-start | bytes 772
  6.5 121.8 %copy-start.3 = (s32[1,64]{1,0:T(1,128)S(1)}, s32[1,64]{1,0:T(1,128)}, u32[]{:S(2)}) copy-start(s32[1,64]{1,0:T(1,128)} %param.11) | copy-start | bytes 772
  6.5 33.1 %all-gather.5.cloned.1.call-start = ((), (), s32[]{:S(2)}) async-start(), calls=%async_computation.1 | async-start | bytes 2359296 | tf_op jit(solution)/shard_map/all_gather | solution.py:161
  7.3 121.0 %all-gather.7.cloned.1.call-start = ((), (), s32[]{:S(2)}) async-start(), calls=%async_computation.2 | async-start | bytes 10485760 | tf_op jit(solution)/shard_map/all_gather | solution.py:162
  40.7 8.1 %all-to-all-start = ((bf16[2,256,256]{2,0,1:T(2,128)(2,1)}), bf16[2,256,256]{2,0,1:T(2,128)(2,1)S(1)}, u32[]{:S(2)}, u32[]{:S(2)}) async-start(bf16[2,256,256]{2,0,1:T(2,128)(2,1)} %bitcast.12), calls=%async_computation | async-start | bytes 524288 | tf_op jit(solution)/shard_map/all_to_all | solution.py:160
  128.3 3.4 %copy-start = (bf16[1,64,256,256]{3,2,1,0:T(8,128)(2,1)S(1)}, bf16[1,64,256,256]{3,2,1,0:T(8,128)(2,1)}, u32[]{:S(2)}) copy-start(bf16[1,64,256,256]{3,2,1,0:T(8,128)(2,1)} %param.8) | copy-start | bytes 25165828
  192.5 1.3 copy-start.1
Sparse Core Ops, SparseCore 0:
  9.0 30.6 all-gather.4
  41.5 86.6 all-gather.6

commit v2 on v1

v2 whole, which is shorter than its diff:
```python
import functools

import jax
import jax.numpy as jnp
from jax import lax
from jax.experimental import pallas as pl
from jax.experimental.pallas import tpu as pltpu
from jax.sharding import PartitionSpec as P

MESH = pl.DeviceIdType.MESH


def pick_blocks(table, index):
    picked = jnp.zeros((index.shape[0],) + table.shape[1:], table.dtype)
    for sector in range(table.shape[0]):
        picked = jnp.where((index == sector)[:, None, None], table[sector][None], picked)
    return picked


def place_kernel(tiles, arr, recv, out, sem):
    @pl.loop(0, tiles)
    def _(s):
        pltpu.make_async_copy(recv.at[arr[s]], out.at[s], sem).start()
    pltpu.make_async_copy(recv, out, sem).wait()


def place(tiles, order):
    smem = pl.BlockSpec(memory_space=pltpu.SMEM)
    hbm = pl.BlockSpec(memory_space=pl.ANY)
    return pl.pallas_call(
        functools.partial(place_kernel, tiles.shape[0]),
        out_shape=jax.ShapeDtypeStruct(tiles.shape, tiles.dtype),
        in_specs=[smem, hbm],
        out_specs=hbm,
        scratch_shapes=[pltpu.SemaphoreType.DMA],
    )(order, tiles)


def many_owners(
    vectors, left_env, right_env, left_sector, right_sector, tile_count, departure, arrival
):
    n_sec = lax.axis_size("sec")
    n_vecs = vectors.shape[0]
    tiles_dev = vectors.shape[1]
    width = vectors.shape[3]
    per_peer = tiles_dev // n_sec
    live = (jnp.arange(tiles_dev, dtype=jnp.int32) < tile_count[0]).astype(jnp.bfloat16)
    masked = vectors * live[None, :, None, None]
    left_blocks = pick_blocks(left_env[0], left_sector[0])
    applied = jnp.einsum(
        "kij,vkjl->vkil", left_blocks, masked, preferred_element_type=jnp.float32
    ).astype(jnp.bfloat16)
    outgoing = place(applied[0], departure[0])
    outgoing = outgoing.reshape(n_vecs, n_sec, per_peer, width, width)
    incoming = lax.all_to_all(outgoing, "sec", split_axis=1, concat_axis=1, tiled=True)
    incoming = incoming.reshape(n_vecs, tiles_dev, width, width)
    placed = place(incoming[0], arrival[0])[None]
    right_blocks = pick_blocks(right_env[0], right_sector[0])
    contrib = jnp.einsum(
        "vkil,kml->vkim", placed, right_blocks, preferred_element_type=jnp.float32
    ).astype(jnp.bfloat16)
    return lax.psum_scatter(contrib, "term", scatter_dimension=2, tiled=True)


def sigma_kernel(
    n_sec, n_term, per_peer, rows, width,
    dep, lsec, cnt, arr, x_hbm, l_src, r_src, sel_src,
    result,
    x, lq, r, a, y, out, recv, sel,
    x_sem, l_send, l_recv, s_send, s_recv, r_send, r_recv, d_recv, o_send, o_recv,
):
    me = lax.axis_index("sec")
    term = lax.axis_index("term")
    z, core = me // 2, me % 2
    tiles = n_sec * per_peer
    load_x = pltpu.make_async_copy(x_hbm, x, x_sem)
    load_x.start()

    chips = (z, z + 1 - 2 * (z % 2), (z + 2) % 4, 3 - z)
    terms = (term, term + 1 - 2 * (term % 2), (term + 2) % 4, 3 - term)
    other = 2 * z + 1 - core

    def to_sec(e):
        return {"sec": e}

    def to_term(t):
        return {"term": t}

    def remote(src, dst, send, recv_sem, device):
        return pltpu.make_async_remote_copy(
            src_ref=src, dst_ref=dst, send_sem=send, recv_sem=recv_sem,
            device_id=device, device_id_type=MESH,
        )

    sent = []

    def start(copy):
        copy.start()
        sent.append(copy)

    def next_send():
        next_send.count += 1
        return r_send.at[next_send.count - 1]

    next_send.count = 0

    def peer(step):
        return lax.rem(me + step, n_sec)

    def block(e):
        return pl.ds(pl.multiple_of(e * per_peer, per_peer), per_peer)

    def quarter(t):
        return pl.ds(pl.multiple_of(t * rows, rows), rows)

    def sel_copy(to, at):
        return remote(sel_src.at[to], sel.at[at], s_send.at[to], s_recv.at[at], to_sec(to))

    def out_copy(to, at):
        return remote(
            out.at[block(to)], recv.at[block(at)], o_send.at[to], o_recv.at[at], to_sec(to)
        )

    def left_copy(to, at):
        return remote(
            l_src.at[:, quarter(to), :], lq.at[:, quarter(at), :],
            l_send.at[to], l_recv.at[at], to_term(to),
        )

    def send_right(t, e, device):
        start(remote(r.at[t, e], r.at[t, e], next_send(), r_recv.at[t, e], device))

    def wait_right(t, e):
        remote(r.at[t, e], r.at[t, e], r_send.at[0], r_recv.at[t, e], to_sec(other)).wait_recv()

    def half_copy(t, e, h, send, device):
        part = r.at[t, e, pl.ds(h * width, width), :]
        return remote(part, part, send, d_recv.at[h, e], device)

    barrier = pltpu.get_barrier_semaphore()
    for step in range(1, n_sec):
        pl.semaphore_signal(barrier, inc=1, device_id=to_sec(peer(step)), device_id_type=MESH)
    for t in terms[1:]:
        pl.semaphore_signal(barrier, inc=1, device_id=to_term(t), device_id_type=MESH)
    r[term, me] = r_src[...]
    lq[:, quarter(term), :] = l_src[:, quarter(term), :]
    sel[me] = sel_src[me]
    pl.semaphore_wait(barrier, n_sec - 1 + n_term - 1)

    for t in terms[1:]:
        left_copy(t, term).start()
    for chip in chips[1:]:
        send_right(term, me, to_sec(2 * chip + core))

    def forward_own(k):
        e = 2 * chips[k] + core
        if k:
            wait_right(term, e)
        for device in (to_term(terms[1]), to_term(terms[2]), to_sec(other)):
            send_right(term, e, device)

    def forward_near(k):
        e = 2 * chips[k] + core
        for h in range(2):
            t = terms[1 + h]
            wait_right(t, e)
            start(half_copy(t, e, h, next_send(), to_term(terms[2 - h])))
            send_right(t, e, to_sec(other))

    def forward_far(k):
        e = 2 * chips[k] + core
        for h in range(2):
            half_copy(terms[3], e, h, r_send.at[0], to_sec(other)).wait_recv()
        send_right(terms[3], e, to_sec(other))

    def left(first, last):
        @pl.loop(first, last, unroll=4)
        def _(p):
            slot = dep[p]
            full = jnp.dot(lq[lsec[slot]], x[slot], preferred_element_type=jnp.float32)
            full = jnp.where(slot < cnt[0], full, 0.0).astype(jnp.bfloat16)
            for t in range(n_term):
                a[t, quarter(p), :] = full[t * rows:(t + 1) * rows]

    def right(e):
        span = pl.ds(pl.multiple_of(e * per_peer * rows, per_peer * rows), per_peer * rows)
        for s in range(2):
            total = None
            for t in range(n_term):
                part = lax.dot_general(
                    a[t, span, :], r[t, e, s * width:(s + 1) * width, :],
                    (((1,), (1,)), ((), ())), preferred_element_type=jnp.float32,
                )
                total = part if total is None else total + part
            y[s] = total

        @pl.loop(0, per_peer, unroll=2)
        def _(i):
            second = sel[e, pl.ds(i, 1), :] == 1
            picked = jnp.where(second, y[1, quarter(i), :], y[0, quarter(i), :])
            out[e * per_peer + i] = picked.astype(jnp.bfloat16)

    def arrived(k):
        e = 2 * chips[k] + 1 - core
        for t in range(n_term):
            wait_right(t, e)

    def stage(k):
        arrived(k)

        @pl.loop(0, 2)
        def _(c):
            e = 2 * chips[k] + c
            sel_copy(e, e).wait_recv()
            right(e)
            out_copy(e, me).start()

    forward_own(0)
    for step in range(1, n_sec):
        sel_copy(peer(step), me).start()
    load_x.wait()
    for t in terms[1:]:
        left_copy(t, t).wait_recv()
    left(0, tiles // 4)
    forward_near(0)
    left(tiles // 4, tiles // 2)
    forward_own(1)
    forward_far(0)
    left(tiles // 2, tiles)
    forward_near(1)
    forward_own(2)
    forward_far(1)
    forward_near(2)
    stage(1)
    forward_own(3)
    forward_far(2)
    forward_near(3)
    stage(2)
    forward_far(3)
    stage(3)
    arrived(0)
    sel_copy(other, other).wait_recv()
    right(other)
    out_copy(other, me).start()
    right(me)
    recv[block(me)] = out[block(me)]

    for step in range(1, n_sec):
        out_copy(peer(step), peer(step)).wait_recv()

    @pl.loop(0, tiles, unroll=4)
    def _(s):
        result[s] = recv[arr[s]]

    for t in terms[1:]:
        left_copy(t, term).wait_send()
    for copy in sent:
        copy.wait_send()
    for step in range(1, n_sec):
        sel_copy(peer(step), me).wait_send()
        out_copy(peer(step), me).wait_send()


def on_device(
    vectors, left_env, right_env, left_sector, right_sector, tile_count, departure, arrival
):
    n_sec = lax.axis_size("sec")
    n_term = lax.axis_size("term")
    tiles = vectors.shape[1]
    width = vectors.shape[3]
    rows = width // n_term
    per_peer = tiles // n_sec
    sectors = left_env.shape[1]

    hits = arrival[0][None, :] == jnp.arange(tiles, dtype=jnp.int32)[:, None]
    chosen = jnp.sum(jnp.where(hits, right_sector[0][None, :], 0), axis=1).astype(jnp.int32)
    chosen = jnp.broadcast_to(chosen.reshape(n_sec, per_peer, 1), (n_sec, per_peer, width))

    vmem = pl.BlockSpec(memory_space=pltpu.VMEM)
    smem = pl.BlockSpec(memory_space=pltpu.SMEM)
    hbm = pl.BlockSpec(memory_space=pl.ANY)
    out = pl.pallas_call(
        functools.partial(sigma_kernel, n_sec, n_term, per_peer, rows, width),
        out_shape=jax.ShapeDtypeStruct((tiles, rows, width), jnp.bfloat16),
        in_specs=[smem, smem, smem, smem, hbm, vmem, vmem, vmem],
        out_specs=vmem,
        scratch_shapes=[
            pltpu.VMEM((tiles, width, width), jnp.bfloat16),
            pltpu.VMEM((sectors, width, width), jnp.bfloat16),
            pltpu.VMEM((n_term, n_sec, sectors * width, width), jnp.bfloat16),
            pltpu.VMEM((n_term, tiles * rows, width), jnp.bfloat16),
            pltpu.VMEM((sectors, per_peer * rows, width), jnp.float32),
            pltpu.VMEM((tiles, rows, width), jnp.bfloat16),
            pltpu.VMEM((tiles, rows, width), jnp.bfloat16),
            pltpu.VMEM((n_sec, per_peer, width), jnp.int32),
            pltpu.SemaphoreType.DMA,
            pltpu.SemaphoreType.DMA((n_term,)),
            pltpu.SemaphoreType.DMA((n_term,)),
            pltpu.SemaphoreType.DMA((n_sec,)),
            pltpu.SemaphoreType.DMA((n_sec,)),
            pltpu.SemaphoreType.DMA((40,)),
            pltpu.SemaphoreType.DMA((n_term, n_sec)),
            pltpu.SemaphoreType.DMA((2, n_sec)),
            pltpu.SemaphoreType.DMA((n_sec,)),
            pltpu.SemaphoreType.DMA((n_sec,)),
        ],
        compiler_params=pltpu.CompilerParams(
            collective_id=0, has_side_effects=True, vmem_limit_bytes=48 * 1024 * 1024
        ),
    )(
        departure[0], left_sector[0], tile_count, arrival[0], vectors[0], left_env[0],
        right_env[0].reshape(sectors * width, width), chosen,
    )
    return out[None]


def solution(mesh):
    in_specs = (
        P(None, "sec", None, None),
        P("term", "sec", None, None),
        P("term", "sec", None, None),
        P("sec", None),
        P("sec", None),
        P("sec"),
        P("sec", None),
        P("sec", None),
    )
    out_specs = P(None, "sec", "term", None)
    small = mesh.shape["sec"] == 8 and mesh.shape["term"] == 4
    body = on_device if small else many_owners
    return jax.shard_map(
        body, mesh=mesh, in_specs=in_specs, out_specs=out_specs, check_vma=False
    )
```

time: 266 us -> 96.5 us (0.36)
  waiting for transfers between devices: 116 us -> 0 us
  Pallas kernels: 126 us -> 89.5 us
  between operations: 14.1 us -> 0.67 us
  starting transfers between devices: 3.48 us -> 0 us
    all_gather x2 -> x0, waiting for transfers between devices: 112 us -> none  [the longest x1 79.4 us: on_device(): r = lax.all_gather(r, 'term', axis=0, tiled=False)]
    pallas_call x2 -> x1, Pallas kernels: 126 us -> 89.5 us  [on_device(): pl.pallas_call(functools.partial(sigma_kernel, n_sec, n_term, per_peer, r...]
    all_to_all x1 -> x0, waiting for transfers between devices: 3.85 us -> none  [on_device(): lax.all_to_all(left_env[0], 'term', split_axis=1, concat_axis=1, tiled=True)]
    all_to_all x1 -> x0, starting transfers between devices: 3.41 us -> none  [on_device(): lax.all_to_all(left_env[0], 'term', split_axis=1, concat_axis=1, tiled=True)]
    unnamed x15 -> x11, local copies, waits for them, and re-layouts: 5.69 us -> 5.21 us
  transfers between devices with their start and end apart: 3 -> 0, of which waited for: 3 -> 0; matrix products, arithmetic and copies ran while one was open for 0% -> 0% of each run, Pallas kernels for 0% -> 0%
where the time goes in v2:
time: 96.5 us; the launch traced here: 96.3 us
  Pallas kernels  89.5 us (93%)
  local copies, waits for them, and re-layouts  5.36 us (6%)
    pallas_call x1, Pallas kernels, on_device(): pl.pallas_call(functools.partial(sigma_kernel, n_sec, n_term, per_peer, r...  89.5 us
    unnamed x11, local copies, waits for them, and re-layouts  5.21 us

profile of v2, /device:TPU:9, one launch (start us, length us, event | category | flops | bytes accessed | tf_op | source)
XLA Modules:
  0.0 96.3 jit_solution(13879952725418617062)
XLA Ops:
  0.7 0.8 select_reduce_fusion
  1.4 0.1 broadcast_in_dim.28
  1.5 0.1 broadcast_in_dim.29.sel_src
  1.6 0.0 copy-start
  1.6 1.0 %copy-done = bf16[1,2,256,256]{3,2,1,0:T(8,128)(2,1)S(1)} copy-done((bf16[1,2,256,256]{3,2,1,0:T(8,128)(2,1)S(1)}, bf16[1,2,256,256]{3,2,1,0:T(8,128)(2,1)}, u32[]{:S(2)}) %copy-start) | copy-done | bytes 262168
  2.6 0.0 copy-start.1
  2.6 0.9 copy-done.1
  3.5 0.0 copy-start.2
  3.5 0.7 copy-done.2
  4.2 0.0 copy-start.3
  4.2 0.7 copy-done.3
  4.8 0.0 copy-start.4
  4.8 0.7 copy-done.4
  5.5 89.5 %shard_map.82 = bf16[64,64,256]{2,1,0:T(8,128)(2,1)S(1)} custom-call(s32[64]{0:T(128)S(1)} %bitcast.11, s32[64]{0:T(128)S(1)} %bitcast.12, s32[1]{0:T(128)S(6)} %copy.10.cnt, s32[64]{0:T(128)S(1)} %bitcast.14, bf16[64,256,256]{2,1,0:T(8,128)(2,1)} %bitcast.15, bf16[2,256,256]{2,1,0:T(8,128)(2,1)S(1)} %bitcast.9, bf16[512,256]{1,0:T(8,128)(2,1)S(1)} %bitcast.10, ...), custom_call_target="tpu_custom_call" | custom-call | tf_op jit(solution)/shard_map/pallas_call | solution.py:282
  95.0 1.3 %copy.11 = bf16[1,64,64,256]{3,2,1,0:T(8,128)(2,1)} copy(bf16[1,64,64,256]{3,2,1,0:T(8,128)(2,1)S(1)} %bitcast.8) | data formatting | bytes 4194304
Async XLA Ops:
  1.6 1.0 %copy-start = (bf16[1,2,256,256]{3,2,1,0:T(8,128)(2,1)S(1)}, bf16[1,2,256,256]{3,2,1,0:T(8,128)(2,1)}, u32[]{:S(2)}) copy-start(bf16[1,2,256,256]{3,2,1,0:T(8,128)(2,1)} %param.9) | copy-start | bytes 786436
  2.6 0.9 copy-start.1
  3.5 0.7 copy-start.2
  4.2 0.7 copy-start.3
  4.8 0.7 copy-start.4
